TPU v7x, 768 devices: a whole 4x8x12 slice. The times are simulated.
768 devices in a mesh: rep: 48 (over z, y_hi), exp: 16 (over y_lo, x, core).
Axes of the slice: x: 4, y: 8 (y_hi: 4, y_lo: 2; y = y_hi * 2 + y_lo), z: 12, core: 2. Of those that a mesh axis runs over, the one named last changes fastest.
Arguments:
- tokens: bfloat16 [2, 1024, 2048], P(None, 'exp'), may hold values from -6 to 6
- cotangent: bfloat16 [2, 1024, 2048], P(None, 'exp'), may hold values from -6 to 6
- expert_ids: int32 [2, 1024, 8], P(None, 'exp'), may hold values from 0 to 127, all different within a row; in each aligned block of 64 rows (0 to 63, 64 to 127, ..., all dimensions but the last counted through in order) at most 8 rows name the same one
- route_probs: bfloat16 [2, 1024, 8], P(None, 'exp'), may hold values from 0.019897461 to 0.5
- gate_weight: bfloat16 [16, 12288, 2048], P('exp', 'rep'), may hold values from -0.125 to 0.125
- up_weight: bfloat16 [16, 12288, 2048], P('exp', 'rep'), may hold values from -0.125 to 0.125
- down_weight: bfloat16 [16, 12288, 2048], P('exp', 'rep'), may hold values from -0.078125 to 0.078125
Outputs:
- grad_tokens: bfloat16 [2, 1024, 2048], P(None, 'exp')
- grad_probs: float32 [2, 1024, 8], P(None, 'exp')
- grad_down: bfloat16 [16, 12288, 2048], P('exp', 'rep')
Inputs may be any that keep to these rules, and one draw needn't show every extreme that they name: `expert_ids`: A token's 8 ids differ. In each aligned block of 64 tokens of one micro-batch no expert is named more than 8 times, a bound that some block reaches.
All inputs are finite; a program needn't handle non-finite values.
Results may differ from a plain program's by a relative error of at most 0.0051.
Values may be sent and summed in bfloat16 or wider, within the bound.
A program may use at most 32 MiB of HBM per device.

v0:
```python
import jax
import jax.numpy as jnp
from jax import lax
from jax.sharding import PartitionSpec as P

FF = 1536
TOPK = 8
EXPERTS = 128
MICRO = 2
CAP = 8


def body(tokens, cotangent, expert_ids, route_probs, gate_weight, up_weight, down_weight):
    group_count = lax.axis_size("exp")
    rep_index = lax.axis_index("rep")
    per_group = EXPERTS // group_count
    hidden_local = gate_weight.shape[1]
    width = tokens.shape[2]
    tok_local = tokens.shape[1]
    held_count = max(1, hidden_local // FF)
    unit_count = hidden_local // held_count
    first_held = rep_index * hidden_local // FF
    slot_count = group_count * held_count * CAP

    def prepare(batch_index):
        flat_ids = expert_ids[batch_index].reshape(-1)
        one_hot = (flat_ids[:, None] == jnp.arange(EXPERTS, dtype=jnp.int32)[None, :]).astype(
            jnp.int32
        )
        before = jnp.cumsum(one_hot, axis=0) - one_hot
        slot_index = jnp.sum(before * one_hot, axis=1)
        local_index = flat_ids % per_group - first_held
        dest_group = flat_ids // per_group
        held_mask = (local_index >= 0) & (local_index < held_count)
        slot_key = jnp.where(
            held_mask, (dest_group * held_count + local_index) * CAP + slot_index, -1
        )
        route_sel = slot_key[None, :] == jnp.arange(slot_count, dtype=jnp.int32)[:, None]
        token_sel = jnp.any(route_sel.reshape(slot_count, tok_local, TOPK), axis=2)
        token_pick = token_sel.astype(jnp.bfloat16)
        send_rows = jnp.dot(
            token_pick, tokens[batch_index], preferred_element_type=jnp.float32
        ).astype(jnp.bfloat16)
        send_cot = jnp.dot(
            token_pick, cotangent[batch_index], preferred_element_type=jnp.float32
        ).astype(jnp.bfloat16)
        send_prob = jnp.dot(
            route_sel.astype(jnp.bfloat16),
            route_probs[batch_index].reshape(-1),
            preferred_element_type=jnp.float32,
        ).astype(jnp.bfloat16)
        send_rows = send_rows.reshape(group_count, held_count * CAP, width)
        send_cot = send_cot.reshape(group_count, held_count * CAP, width)
        send_prob = send_prob.reshape(group_count, held_count * CAP)
        return (
            send_rows,
            send_cot,
            send_prob,
            route_sel.astype(jnp.float32),
            token_sel.astype(jnp.float32),
        )

    prepared = [prepare(batch_index) for batch_index in range(MICRO)]
    down_total = jnp.zeros((held_count, unit_count, width), jnp.float32)
    local_sums = []
    for batch_index in range(MICRO):
        send_rows, send_cot, send_prob, route_sel, token_sel = prepared[batch_index]
        recv_rows, recv_cot, recv_prob = (
            lax.all_to_all(send_rows, "exp", split_axis=0, concat_axis=0, tiled=True),
            lax.all_to_all(send_cot, "exp", split_axis=0, concat_axis=0, tiled=True),
            lax.all_to_all(send_prob, "exp", split_axis=0, concat_axis=0, tiled=True),
        )
        rows = recv_rows.reshape(group_count, 1, held_count, CAP, width)
        cots = recv_cot.reshape(group_count, 1, held_count, CAP, width)
        probs = recv_prob.reshape(group_count, 1, held_count, CAP).astype(jnp.float32)[..., None]
        gate_pre = jnp.einsum(
            "sbncd,nud->sbncu", rows, gate_weight, preferred_element_type=jnp.float32
        )
        up_pre = jnp.einsum("sbncd,nud->sbncu", rows, up_weight, preferred_element_type=jnp.float32)
        act_grad = jnp.einsum(
            "sbncd,nud->sbncu", cots, down_weight, preferred_element_type=jnp.float32
        )
        sigmoid_gate = jax.nn.sigmoid(gate_pre)
        silu_gate = gate_pre * sigmoid_gate
        act = silu_gate * up_pre
        prob_part = jnp.sum(act * act_grad, axis=-1)
        weighted_act = (probs * act).astype(jnp.bfloat16)
        scaled = probs * act_grad
        gate_grad = (
            scaled * up_pre * sigmoid_gate * (1.0 + gate_pre * (1.0 - sigmoid_gate))
        ).astype(jnp.bfloat16)
        up_grad = (scaled * silu_gate).astype(jnp.bfloat16)
        row_part = jnp.einsum(
            "sbncu,nud->sbncd", gate_grad, gate_weight, preferred_element_type=jnp.float32
        )
        row_part = row_part + jnp.einsum(
            "sbncu,nud->sbncd", up_grad, up_weight, preferred_element_type=jnp.float32
        )
        down_term = jnp.einsum(
            "sbncu,sbncd->nud", weighted_act, cots, preferred_element_type=jnp.float32
        )
        row_part = row_part.reshape(group_count, 1 * held_count * CAP, width)
        prob_part = prob_part.reshape(group_count, 1 * held_count * CAP)
        row_part, prob_part, down_term = (row_part, prob_part, down_term)
        down_total = down_total + down_term
        back_rows, back_prob = (
            lax.all_to_all(row_part, "exp", split_axis=0, concat_axis=0, tiled=True),
            lax.all_to_all(prob_part, "exp", split_axis=0, concat_axis=0, tiled=True),
        )
        finish_row_total = jnp.dot(
            token_sel.T, back_rows.reshape(slot_count, width), precision=lax.Precision.HIGHEST
        )
        finish_prob_total = jnp.dot(
            route_sel.T, back_prob.reshape(slot_count), precision=lax.Precision.HIGHEST
        )
        local_sums.append((finish_row_total, finish_prob_total.reshape(tok_local, TOPK)))
    row_sums = []
    prob_sums = []
    for batch_index in range(MICRO):
        row_total, prob_total = lax.psum(
            (local_sums[batch_index][0], local_sums[batch_index][1]), "rep"
        )
        row_sums.append(row_total)
        prob_sums.append(prob_total)
    grad_rows = jnp.stack(row_sums, axis=0)
    grad_probs = jnp.stack(prob_sums, axis=0)
    grad_tokens = grad_rows.astype(jnp.bfloat16)
    grad_down = down_total.astype(jnp.bfloat16)
    return (grad_tokens, grad_probs, grad_down)


def solution(mesh):
    return jax.shard_map(
        body,
        mesh=mesh,
        in_specs=(
            P(None, "exp", None),
            P(None, "exp", None),
            P(None, "exp", None),
            P(None, "exp", None),
            P("exp", "rep", None),
            P("exp", "rep", None),
            P("exp", "rep", None),
        ),
        out_specs=(P(None, "exp", None), P(None, "exp", None), P("exp", "rep", None)),
        check_vma=False,
    )
```

profile of v0, /device:TPU:8, one launch (start us, length us, event | category | flops | bytes accessed | tf_op | source)
XLA Modules:
  0.0 406.0 jit_solution(4655734014752167820)
XLA Ops:
  5.2 12.8 %all-to-all-start = ((bf16[16,1,8]{2,1,0:T(2,128)(2,1)}), bf16[16,1,8]{2,1,0:T(2,128)(2,1)S(1)}, u32[]{:S(2)}, u32[]{:S(2)}) async-start(bf16[16,1,8]{2,1,0:T(2,128)(2,1)} %all_to_all.56), calls=%async_computation | async-start | bytes 16384 | tf_op jit(solution)/shard_map/all_to_all | solution.py:71
  19.4 3.2 all-to-all-done
  22.6 4.9 %all-to-all-start.6 = ((bf16[16,8,2048]{2,1,0:T(8,128)(2,1)}), bf16[16,8,2048]{2,1,0:T(8,128)(2,1)S(1)}, u32[]{:S(2)}, u32[]{:S(2)}) async-start(bf16[16,8,2048]{2,1,0:T(8,128)(2,1)} %fusion.6), calls=%async_computation.6 | async-start | bytes 1048576 | tf_op jit(solution)/shard_map/all_to_all | solution.py:69
  28.6 8.4 %all-to-all-done.6 = bf16[16,8,2048]{2,1,0:T(8,128)(2,1)S(1)} async-done(((bf16[16,8,2048]{2,1,0:T(8,128)(2,1)}), bf16[16,8,2048]{2,1,0:T(8,128)(2,1)S(1)}, u32[]{:S(2)}, u32[]{:S(2)}) %all-to-all-start.6) | async-done | bytes 524320 | tf_op jit(solution)/shard_map/all_to_all | solution.py:69
  37.0 4.9 %all-to-all-start.5 = ((bf16[16,8,2048]{2,1,0:T(8,128)(2,1)}), bf16[16,8,2048]{2,1,0:T(8,128)(2,1)S(1)}, u32[]{:S(2)}, u32[]{:S(2)}) async-start(bf16[16,8,2048]{2,1,0:T(8,128)(2,1)} %fusion.5), calls=%async_computation.5 | async-start | bytes 1048576 | tf_op jit(solution)/shard_map/all_to_all | solution.py:70
  43.4 8.1 %all-to-all-done.5 = bf16[16,8,2048]{2,1,0:T(8,128)(2,1)S(1)} async-done(((bf16[16,8,2048]{2,1,0:T(8,128)(2,1)}), bf16[16,8,2048]{2,1,0:T(8,128)(2,1)S(1)}, u32[]{:S(2)}, u32[]{:S(2)}) %all-to-all-start.5) | async-done | bytes 524320 | tf_op jit(solution)/shard_map/all_to_all | solution.py:70
  52.2 4.9 %all-to-all-start.2 = ((bf16[16,8,2048]{2,1,0:T(8,128)(2,1)}), bf16[16,8,2048]{2,1,0:T(8,128)(2,1)S(1)}, u32[]{:S(2)}, u32[]{:S(2)}) async-start(bf16[16,8,2048]{2,1,0:T(8,128)(2,1)} %fusion.4), calls=%async_computation.2 | async-start | bytes 1048576 | tf_op jit(solution)/shard_map/all_to_all | solution.py:69
  58.2 2.1 fusion.3
  60.3 6.3 %all-to-all-done.2 = bf16[16,8,2048]{2,1,0:T(8,128)(2,1)S(1)} async-done(((bf16[16,8,2048]{2,1,0:T(8,128)(2,1)}), bf16[16,8,2048]{2,1,0:T(8,128)(2,1)S(1)}, u32[]{:S(2)}, u32[]{:S(2)}) %all-to-all-start.2) | async-done | bytes 524320 | tf_op jit(solution)/shard_map/all_to_all | solution.py:69
  66.6 5.5 %all-to-all-start.1 = ((bf16[16,8,2048]{2,1,0:T(8,128)(2,1)}), bf16[16,8,2048]{2,1,0:T(8,128)(2,1)}, u32[]{:S(2)}, u32[]{:S(2)}) async-start(bf16[16,8,2048]{2,1,0:T(8,128)(2,1)} %fusion.3), calls=%async_computation.1 | async-start | bytes 1048576 | tf_op jit(solution)/shard_map/all_to_all | solution.py:70
  76.9 4.8 %all-to-all-done.1 = bf16[16,8,2048]{2,1,0:T(8,128)(2,1)} async-done(((bf16[16,8,2048]{2,1,0:T(8,128)(2,1)}), bf16[16,8,2048]{2,1,0:T(8,128)(2,1)}, u32[]{:S(2)}, u32[]{:S(2)}) %all-to-all-start.1) | async-done | bytes 524320 | tf_op jit(solution)/shard_map/all_to_all | solution.py:70
  81.7 5.3 %all-to-all-start.4 = ((bf16[16,1,8]{2,1,0:T(2,128)(2,1)}), bf16[16,1,8]{2,1,0:T(2,128)(2,1)}, u32[]{:S(2)}, u32[]{:S(2)}) async-start(bf16[16,1,8]{2,1,0:T(2,128)(2,1)} %all_to_all.57), calls=%async_computation.4 | async-start | bytes 16384 | tf_op jit(solution)/shard_map/all_to_all | solution.py:71
  87.1 2.8 multiply_reduce_fusion.1
  91.7 5.4 %all-to-all-start.9 = ((f32[16,1,8]{2,1,0:T(1,128)}), f32[16,1,8]{2,1,0:T(1,128)}, u32[]{:S(2)}, u32[]{:S(2)}) async-start(f32[16,1,8]{2,1,0:T(1,128)} %bitcast.252), calls=%async_computation.9 | async-start | bytes 16384 | tf_op jit(solution)/shard_map/all_to_all | solution.py:108
  98.3 3.4 all-to-all-done.9
  101.8 5.2 %all-to-all-start.8 = ((f32[16,1,8]{2,1,0:T(1,128)}), f32[16,1,8]{2,1,0:T(1,128)}, u32[]{:S(2)}, u32[]{:S(2)}) async-start(f32[16,1,8]{2,1,0:T(1,128)} %bitcast.253), calls=%async_computation.8 | async-start | bytes 16384 | tf_op jit(solution)/shard_map/all_to_all | solution.py:108
  107.0 2.2 convolution_add_fusion.1
  109.2 2.4 all-to-all-done.8
  111.6 5.0 %all-to-all-start.3 = ((f32[16,8,2048]{2,1,0:T(8,128)}), f32[16,8,2048]{2,1,0:T(8,128)S(1)}, u32[]{:S(2)}, u32[]{:S(2)}) async-start(f32[16,8,2048]{2,1,0:T(8,128)} %convolution_add_fusion.1), calls=%async_computation.3 | async-start | bytes 2097152 | tf_op jit(solution)/shard_map/all_to_all | solution.py:107
  123.2 8.6 %all-to-all-done.3 = f32[16,8,2048]{2,1,0:T(8,128)S(1)} async-done(((f32[16,8,2048]{2,1,0:T(8,128)}), f32[16,8,2048]{2,1,0:T(8,128)S(1)}, u32[]{:S(2)}, u32[]{:S(2)}) %all-to-all-start.3) | async-done | bytes 1048608 | tf_op jit(solution)/shard_map/all_to_all | solution.py:107
  131.8 5.0 %all-to-all-start.7 = ((f32[16,8,2048]{2,1,0:T(8,128)}), f32[16,8,2048]{2,1,0:T(8,128)S(1)}, u32[]{:S(2)}, u32[]{:S(2)}) async-start(f32[16,8,2048]{2,1,0:T(8,128)} %convolution_add_fusion), calls=%async_computation.7 | async-start | bytes 2097152 | tf_op jit(solution)/shard_map/all_to_all | solution.py:107
  138.5 2.6 fusion.2
  149.8 2.2 all-to-all-done.7
  152.5 252.1 %all-reduce.2 = (bf16[64,2048]{1,0:T(8,128)(2,1)S(1)}, bf16[64,2048]{1,0:T(8,128)(2,1)S(1)}, f32[1,64,8]{1,2,0:T(8,128)S(1)}, f32[1,64,8]{1,2,0:T(8,128)S(1)}) all-reduce(f32[64,2048]{1,0:T(8,128)S(1)} %fusion.9, f32[64,2048]{1,0:T(8,128)} %fusion.11, f32[1,64,8]{1,2,0:T(8,128)S(1)} %copy.79, ...), channel_id=1, replica_groups=mesh['rep'=48,'exp'=16] {'rep'}, use_global_device_ids=true, to_apply=%region_9.10 | all-reduce | flops 263168 | bytes 1581056 | tf_op jit(solution)/shard_map/psum | solution.py:120
  (105 shorter events, 37.2 us)
Async XLA Ops:
  0.6 72.2 %copy-start = (bf16[1,256,2048]{2,1,0:T(8,128)(2,1)S(1)}, bf16[1,256,2048]{2,1,0:T(8,128)(2,1)}, u32[]{:S(2)}) copy-start(bf16[1,256,2048]{2,1,0:T(8,128)(2,1)} %param.11) | copy-start | bytes 3145732
  0.6 17.6 %copy-start.8 = (bf16[2,64,2048]{2,1,0:T(8,128)(2,1)S(1)}, bf16[2,64,2048]{2,1,0:T(8,128)(2,1)}, u32[]{:S(2)}) copy-start(bf16[2,64,2048]{2,1,0:T(8,128)(2,1)} %param.7) | copy-start | bytes 1572868
  3.5 24.0 %copy-start.9 = (bf16[2,64,2048]{2,1,0:T(8,128)(2,1)S(1)}, bf16[2,64,2048]{2,1,0:T(8,128)(2,1)}, u32[]{:S(2)}) copy-start(bf16[2,64,2048]{2,1,0:T(8,128)(2,1)} %param.8) | copy-start | bytes 1572868
  5.2 17.4 %all-to-all-start = ((bf16[16,1,8]{2,1,0:T(2,128)(2,1)}), bf16[16,1,8]{2,1,0:T(2,128)(2,1)S(1)}, u32[]{:S(2)}, u32[]{:S(2)}) async-start(bf16[16,1,8]{2,1,0:T(2,128)(2,1)} %all_to_all.56), calls=%async_computation | async-start | bytes 16384 | tf_op jit(solution)/shard_map/all_to_all | solution.py:71
  18.1 25.2 %copy-start.10 = (s32[64,8]{1,0:T(8,128)}, s32[64,8]{1,0:T(8,128)S(1)}, u32[]{:S(2)}) copy-start(s32[64,8]{1,0:T(8,128)S(1)} %fusion.84) | copy-start | bytes 6148
  22.6 14.4 %all-to-all-start.6 = ((bf16[16,8,2048]{2,1,0:T(8,128)(2,1)}), bf16[16,8,2048]{2,1,0:T(8,128)(2,1)S(1)}, u32[]{:S(2)}, u32[]{:S(2)}) async-start(bf16[16,8,2048]{2,1,0:T(8,128)(2,1)} %fusion.6), calls=%async_computation.6 | async-start | bytes 1048576 | tf_op jit(solution)/shard_map/all_to_all | solution.py:69
  37.0 14.4 %all-to-all-start.5 = ((bf16[16,8,2048]{2,1,0:T(8,128)(2,1)}), bf16[16,8,2048]{2,1,0:T(8,128)(2,1)S(1)}, u32[]{:S(2)}, u32[]{:S(2)}) async-start(bf16[16,8,2048]{2,1,0:T(8,128)(2,1)} %fusion.5), calls=%async_computation.5 | async-start | bytes 1048576 | tf_op jit(solution)/shard_map/all_to_all | solution.py:70
  42.0 31.2 %copy-start.12 = (s32[64,8]{1,0:T(8,128)}, s32[64,8]{1,0:T(8,128)S(1)}, u32[]{:S(2)}) copy-start(s32[64,8]{1,0:T(8,128)S(1)} %fusion.79) | copy-start | bytes 6148
  52.2 14.4 %all-to-all-start.2 = ((bf16[16,8,2048]{2,1,0:T(8,128)(2,1)}), bf16[16,8,2048]{2,1,0:T(8,128)(2,1)S(1)}, u32[]{:S(2)}, u32[]{:S(2)}) async-start(bf16[16,8,2048]{2,1,0:T(8,128)(2,1)} %fusion.4), calls=%async_computation.2 | async-start | bytes 1048576 | tf_op jit(solution)/shard_map/all_to_all | solution.py:69
  57.1 16.2 %copy-start.1 = (bf16[1,256,2048]{2,1,0:T(8,128)(2,1)S(1)}, bf16[1,256,2048]{2,1,0:T(8,128)(2,1)}, u32[]{:S(2)}) copy-start(bf16[1,256,2048]{2,1,0:T(8,128)(2,1)} %param.12) | copy-start | bytes 3145732
  66.6 15.1 %all-to-all-start.1 = ((bf16[16,8,2048]{2,1,0:T(8,128)(2,1)}), bf16[16,8,2048]{2,1,0:T(8,128)(2,1)}, u32[]{:S(2)}, u32[]{:S(2)}) async-start(bf16[16,8,2048]{2,1,0:T(8,128)(2,1)} %fusion.3), calls=%async_computation.1 | async-start | bytes 1048576 | tf_op jit(solution)/shard_map/all_to_all | solution.py:70
  73.8 1.3 copy-start.2
  73.8 1.4 copy-start.5
  75.2 11.9 %copy-start.3 = (bf16[1,256,2048]{2,1,0:T(8,128)(2,1)S(1)}, bf16[1,256,2048]{2,1,0:T(8,128)(2,1)}, u32[]{:S(2)}) copy-start(bf16[1,256,2048]{2,1,0:T(8,128)(2,1)} %param.13) | copy-start | bytes 3145732
  81.7 9.9 %all-to-all-start.4 = ((bf16[16,1,8]{2,1,0:T(2,128)(2,1)}), bf16[16,1,8]{2,1,0:T(2,128)(2,1)}, u32[]{:S(2)}, u32[]{:S(2)}) async-start(bf16[16,1,8]{2,1,0:T(2,128)(2,1)} %all_to_all.57), calls=%async_computation.4 | async-start | bytes 16384 | tf_op jit(solution)/shard_map/all_to_all | solution.py:71
  91.7 10.1 %all-to-all-start.9 = ((f32[16,1,8]{2,1,0:T(1,128)}), f32[16,1,8]{2,1,0:T(1,128)}, u32[]{:S(2)}, u32[]{:S(2)}) async-start(f32[16,1,8]{2,1,0:T(1,128)} %bitcast.252), calls=%async_computation.9 | async-start | bytes 16384 | tf_op jit(solution)/shard_map/all_to_all | solution.py:108
  101.8 9.8 %all-to-all-start.8 = ((f32[16,1,8]{2,1,0:T(1,128)}), f32[16,1,8]{2,1,0:T(1,128)}, u32[]{:S(2)}, u32[]{:S(2)}) async-start(f32[16,1,8]{2,1,0:T(1,128)} %bitcast.253), calls=%async_computation.8 | async-start | bytes 16384 | tf_op jit(solution)/shard_map/all_to_all | solution.py:108
  111.6 20.2 %all-to-all-start.3 = ((f32[16,8,2048]{2,1,0:T(8,128)}), f32[16,8,2048]{2,1,0:T(8,128)S(1)}, u32[]{:S(2)}, u32[]{:S(2)}) async-start(f32[16,8,2048]{2,1,0:T(8,128)} %convolution_add_fusion.1), calls=%async_computation.3 | async-start | bytes 2097152 | tf_op jit(solution)/shard_map/all_to_all | solution.py:107
  120.5 1.4 copy-start.7
  120.5 1.4 copy-start.15
  131.8 20.2 %all-to-all-start.7 = ((f32[16,8,2048]{2,1,0:T(8,128)}), f32[16,8,2048]{2,1,0:T(8,128)S(1)}, u32[]{:S(2)}, u32[]{:S(2)}) async-start(f32[16,8,2048]{2,1,0:T(8,128)} %convolution_add_fusion), calls=%async_computation.7 | async-start | bytes 2097152 | tf_op jit(solution)/shard_map/all_to_all | solution.py:107
  136.8 1.7 copy-start.14
  138.5 4.6 %copy-start.11 = (s32[64,8]{1,0:T(8,128)S(1)}, s32[64,8]{1,0:T(8,128)}, u32[]{:S(2)}) copy-start(s32[64,8]{1,0:T(8,128)} %copy-done.10) | copy-start | bytes 6148
  138.5 8.0 %copy-start.13 = (s32[64,8]{1,0:T(8,128)S(1)}, s32[64,8]{1,0:T(8,128)}, u32[]{:S(2)}) copy-start(s32[64,8]{1,0:T(8,128)} %copy-done.12) | copy-start | bytes 6148
  (2 other events, 1.8 us)
where the time goes:
time: 407 us; the launch traced here: 406 us
  blocking collectives  252 us (62%)
  starting transfers between devices  58.9 us (14%)
  waiting for transfers between devices  49.1 us (12%)
  matrix products  28.3 us (7%)
  local copies, waits for them, and re-layouts  9.82 us (2%)
  other arithmetic  6.89 us (2%)
    psum x1, blocking collectives, body(): lax.psum((local_sums[batch_index][0], local_sums[batch_index][1]), 'rep')  252 us
    all_to_all x2, starting transfers between devices, body(): lax.all_to_all(send_prob, 'exp', split_axis=0, concat_axis=0, tiled=True)  18.1 us
    all_to_all x2, waiting for transfers between devices, body(): lax.all_to_all(send_rows, 'exp', split_axis=0, concat_axis=0, tiled=True)  14.6 us
    all_to_all x2, waiting for transfers between devices, body(): lax.all_to_all(send_cot, 'exp', split_axis=0, concat_axis=0, tiled=True)  12.9 us
    all_to_all x2, waiting for transfers between devices, body(): lax.all_to_all(row_part, 'exp', split_axis=0, concat_axis=0, tiled=True)  10.8 us
    all_to_all x2, starting transfers between devices, body(): lax.all_to_all(prob_part, 'exp', split_axis=0, concat_axis=0, tiled=True)  10.6 us
    all_to_all x2, starting transfers between devices, body(): lax.all_to_all(send_cot, 'exp', split_axis=0, concat_axis=0, tiled=True)  10.4 us
    all_to_all x2, starting transfers between devices, body(): lax.all_to_all(row_part, 'exp', split_axis=0, concat_axis=0, tiled=True)  10 us
  transfers between devices with their start and end apart: 10, of which 10 were waited for; matrix products, arithmetic and copies ran while one was open for 9% of the time, Pallas kernels for 0%

commit v1 on v0

v1 whole, which is shorter than its diff:
```python
import functools

import jax
import jax.numpy as jnp
from jax import lax
from jax.experimental import pallas as pl
from jax.experimental.pallas import tpu as pltpu
from jax.sharding import PartitionSpec as P

MESH = pl.DeviceIdType.MESH
FF = 1536
TOPK = 8
EXPERTS = 128
MICRO = 2
CAP = 8
N_EXP = 16
N_Z = 12
N_Y = 4
PER_GROUP = EXPERTS // N_EXP
TOK = 64
D = 2048
UNITS = 256
WIDE = D + 128
HALF = 1152
CHUNK_ROWS = 32
CHUNK_COLS = 384
BF16 = jnp.bfloat16
F32 = jnp.float32


def flip(a, d):
    out = 0
    for bit in (1, 2, 4, 8):
        out = out + ((a // bit + d // bit) % 2) * bit
    return out


def kernel(
    tok_ref, cot_ref, ids_ref, probs_ref, gate_hbm, up_hbm, down_hbm,
    gtok_ref, gprob_ref, gdown_ref,
    weights, pick, send_f, recv_f, send_r, recv_r, red, recv_z, part_y, fin, gdown, wact_buf,
    w_sem, out_sem, sf_sem, rf_sem, sr_sem, rr_sem, sz_sem, rz_sem, sy_sem, ry_sem, sg_sem, rg_sem,
):
    rep = lax.axis_index("rep")
    me = lax.axis_index("exp")
    z = rep // N_Y
    y_hi = rep % N_Y
    y_lo = me // 8

    def local_expert(r):
        return r * UNITS // FF

    def rep_of(m, d):
        if m == 0:
            return rep
        step = (d // 8) * (2 * y_lo - 1)
        return z * N_Y + (y_hi + step + N_Y) % N_Y

    def exp_peer(m, p):
        d = p + 1
        return (rep_of(m, d), flip(me, d))

    def z_peer(q):
        return (((z + q + 1) % N_Z) * N_Y + y_hi, me)

    def y_peer(q):
        return (z * N_Y + (y_hi + q + 1) % N_Y, me)

    weight_copies = [
        pltpu.make_async_copy(src, weights.at[pl.ds(UNITS * i, UNITS)], w_sem.at[i])
        for i, src in enumerate((gate_hbm, up_hbm, down_hbm))
    ]
    for copy in weight_copies:
        copy.start()

    barrier = pltpu.get_barrier_semaphore()

    def greet(device):
        pl.semaphore_signal(barrier, inc=1, device_id=device, device_id_type=MESH)

    @pl.loop(0, N_EXP - 1)
    def _(p):
        greet(exp_peer(0, p))

    @pl.loop(0, 8)
    def _(p):
        greet(exp_peer(1, p + 7))

    @pl.loop(0, N_Z - 1)
    def _(q):
        greet(z_peer(q))

    @pl.loop(0, N_Y - 1)
    def _(q):
        greet(y_peer(q))

    greeted = (N_EXP - 1) + 8 + (N_Z - 1) + (N_Y - 1)

    lane = lax.broadcasted_iota(jnp.int32, (1, 256), 1)
    lane_d = (lane // 16 + 1) % 16
    lane_half = (lane // 8) % 2
    lane_slot = (lane % 8).astype(F32)
    lane_exp = flip(me, lane_d)
    expert_lane = lax.broadcasted_iota(jnp.int32, (1, EXPERTS), 1)
    tri = (
        lax.broadcasted_iota(jnp.int32, (TOK, TOK), 0)
        > lax.broadcasted_iota(jnp.int32, (TOK, TOK), 1)
    ).astype(BF16)

    def prepare(m):
        ids = ids_ref[m]
        probs = probs_ref[m].astype(F32)
        if m == 0:
            group = local_expert(rep)
        else:
            near, far = local_expert(rep), local_expert(rep_of(1, 8))
            group = near + (lane_d // 8) * (far - near)
        lane_expert = lane_exp * PER_GROUP + group
        member = jnp.zeros((TOK, 256), F32)
        table = jnp.zeros((TOK, EXPERTS), F32)
        for k in range(TOPK):
            column = ids[:, k : k + 1]
            member = member + jnp.where(column == lane_expert, 1.0, 0.0)
            table = table + jnp.where(column == expert_lane, probs[:, k : k + 1], 0.0)
        before = jnp.dot(tri, member.astype(BF16), preferred_element_type=F32)
        one_hot = jnp.where(before == lane_slot, member, 0.0)
        first = jnp.where(lane_half == 0, one_hot, 0.0)
        second = jnp.where(lane_half == 1, one_hot, 0.0)
        pick[m] = jnp.concatenate([first, second], axis=0).astype(BF16)
        rows = jnp.concatenate([tok_ref[m], cot_ref[m]], axis=0)
        table = table.astype(BF16)
        tables = jnp.concatenate([table, table], axis=0)
        chosen = pick[m]
        for start, size, source in ((0, 1024, rows[:, :1024]), (1024, 1024, rows[:, 1024:]), (D, 128, tables)):
            out = lax.dot_general(
                chosen, source, (((0,), (0,)), ((), ())), preferred_element_type=F32
            ).astype(BF16).reshape(16, 16, size)
            send_f[m, :, :, start : start + size] = out[:15]
            recv_f[m, 15, :, start : start + size] = out[15]

    def start_all(count, src, dst, send_sem, recv_sem, peer):
        @pl.loop(0, count)
        def _(i):
            pltpu.make_async_remote_copy(
                src_ref=src(i), dst_ref=dst(i), send_sem=send_sem, recv_sem=recv_sem,
                device_id=peer(i), device_id_type=MESH,
            ).start()

    def wait_for(ref, sem):
        pltpu.make_async_copy(ref, ref, sem).wait()

    def send_forward(m):
        start_all(
            15, lambda p: send_f.at[m, p], lambda p: recv_f.at[m, p],
            sf_sem.at[m], rf_sem.at[m], functools.partial(exp_peer, m),
        )

    def compute(m):
        rows = recv_f[m].reshape(256, WIDE)
        pre = lax.dot_general(
            rows[:, :D], weights[...], (((1,), (1,)), ((), ())), preferred_element_type=F32
        ).reshape(16, 2, 8, 3 * UNITS)
        gate_pre = pre[:, 0, :, :UNITS].reshape(128, UNITS)
        up_pre = pre[:, 0, :, UNITS : 2 * UNITS].reshape(128, UNITS)
        act_grad = pre[:, 1, :, 2 * UNITS :].reshape(128, UNITS)
        mine = (expert_lane == me * PER_GROUP + local_expert(rep)).astype(F32)
        prob = rows[:, D:].astype(F32).reshape(16, 2, 8, 128)[:, 0].reshape(128, 128)
        prob = jnp.sum(prob * mine, axis=1, keepdims=True)
        sigmoid_gate = jax.nn.sigmoid(gate_pre)
        silu_gate = gate_pre * sigmoid_gate
        act = silu_gate * up_pre
        prob_part = jnp.sum(act * act_grad, axis=1, keepdims=True)
        wact = (prob * act).reshape(16, 1, 8, UNITS)
        scaled = prob * act_grad
        gate_grad = scaled * up_pre * sigmoid_gate * (1.0 + gate_pre * (1.0 - sigmoid_gate))
        up_grad = scaled * silu_gate
        wact_buf[m] = (
            jnp.concatenate([jnp.zeros_like(wact), wact], axis=1).reshape(256, UNITS).astype(BF16)
        )
        grads = jnp.concatenate([gate_grad, up_grad], axis=1).astype(BF16)
        left = jnp.dot(grads, weights[: 2 * UNITS, :HALF], preferred_element_type=F32)
        right = jnp.dot(grads, weights[: 2 * UNITS, HALF:], preferred_element_type=F32)
        right = jnp.concatenate([right, prob_part * mine, jnp.zeros((128, 128), F32)], axis=1)
        out = jnp.concatenate(
            [left.reshape(16, 8, HALF), right.reshape(16, 8, HALF)], axis=1
        ).astype(BF16)
        send_r[m] = out[:15]
        recv_r[m, 15] = out[15]

    def send_back(m):
        start_all(
            15, lambda p: send_r.at[m, p], lambda p: recv_r.at[m, p],
            sr_sem.at[m], rr_sem.at[m], functools.partial(exp_peer, m),
        )

    def combine(m):
        total = jnp.dot(
            pick[m], recv_r[m].reshape(256, HALF), preferred_element_type=F32
        ).astype(BF16)
        for c in range(N_Z):
            i, j = c // 3, c % 3
            red[m, c] = total[
                CHUNK_ROWS * i : CHUNK_ROWS * (i + 1), CHUNK_COLS * j : CHUNK_COLS * (j + 1)
            ]

    def send_z(m):
        start_all(
            N_Z - 1, lambda q: red.at[m, (z + q + 1) % N_Z], lambda q: recv_z.at[m, q],
            sz_sem.at[m], rz_sem.at[m], z_peer,
        )

    def sum_z(m):
        total = red[m, z].astype(F32)
        for q in range(N_Z - 1):
            total = total + recv_z[m, q].astype(F32)
        part_y[m, y_hi] = total.astype(BF16)

    def send_y(m):
        start_all(
            N_Y - 1, lambda q: part_y.at[m, y_hi], lambda q: part_y.at[m, y_hi],
            sy_sem.at[m], ry_sem.at[m], y_peer,
        )

    def sum_y(m):
        total = part_y[m, 0].astype(F32)
        for q in range(1, N_Y):
            total = total + part_y[m, q].astype(F32)
        fin[m, z] = total.astype(BF16)

    def send_out(m):
        start_all(
            N_Z - 1, lambda q: fin.at[m, z], lambda q: fin.at[m, z],
            sg_sem.at[m], rg_sem.at[m], z_peer,
        )

    def finish(m):
        for c in range(N_Z):
            i, j = c // 3, c % 3
            row = CHUNK_ROWS * (i % 2)
            col = HALF * (i // 2) + CHUNK_COLS * j
            size = min(CHUNK_COLS, D - col)
            gtok_ref[m, row : row + CHUNK_ROWS, col : col + size] = fin[m, c, :, :size]
        ids = ids_ref[m]
        table = jnp.concatenate(
            [fin[m, 8, :, 128:256], fin[m, 11, :, 128:256]], axis=0
        ).astype(F32)
        columns = [
            jnp.sum(jnp.where(ids[:, k : k + 1] == expert_lane, table, 0.0), axis=1, keepdims=True)
            for k in range(TOPK)
        ]
        gprob_ref[m] = jnp.concatenate(columns, axis=1)

    prepare(0)
    pl.semaphore_wait(barrier, greeted)
    send_forward(0)
    prepare(1)
    send_forward(1)
    for copy in weight_copies:
        copy.wait()

    wait_for(recv_f.at[0, pl.ds(0, 15)], rf_sem.at[0])
    compute(0)
    send_back(0)
    wait_for(recv_f.at[1, pl.ds(0, 15)], rf_sem.at[1])
    compute(1)
    send_back(1)

    acts = wact_buf[...].reshape(512, UNITS)
    for part in range(4):
        cols = slice(512 * part, 512 * (part + 1))
        gdown[:, cols] = lax.dot_general(
            acts, recv_f[:, :, :, cols].reshape(512, 512), (((0,), (0,)), ((), ())),
            preferred_element_type=F32,
        ).astype(BF16)
    out_copy = pltpu.make_async_copy(gdown, gdown_ref, out_sem)
    out_copy.start()

    wait_for(recv_r.at[0, pl.ds(0, 15)], rr_sem.at[0])
    combine(0)
    send_z(0)
    wait_for(recv_r.at[1, pl.ds(0, 15)], rr_sem.at[1])
    combine(1)
    send_z(1)
    for m in range(MICRO):
        wait_for(recv_z.at[m], rz_sem.at[m])
        sum_z(m)
        send_y(m)
        wait_for(part_y.at[m, pl.ds(0, N_Y - 1)], ry_sem.at[m])
        sum_y(m)
        send_out(m)
    for m in range(MICRO):
        wait_for(fin.at[m, pl.ds(0, N_Z - 1)], rg_sem.at[m])
        finish(m)
    out_copy.wait()
    for m in range(MICRO):
        wait_for(send_f.at[m], sf_sem.at[m])
        wait_for(send_r.at[m], sr_sem.at[m])
        wait_for(recv_z.at[m], sz_sem.at[m])
        wait_for(part_y.at[m, pl.ds(0, N_Y - 1)], sy_sem.at[m])
        wait_for(fin.at[m, pl.ds(0, N_Z - 1)], sg_sem.at[m])


def body(tokens, cotangent, expert_ids, route_probs, gate_weight, up_weight, down_weight):
    vmem = pl.BlockSpec(memory_space=pltpu.VMEM)
    hbm = pl.BlockSpec(memory_space=pl.ANY)
    gtok, gprob, gdown = pl.pallas_call(
        kernel,
        name="expert_backward",
        out_shape=(
            jax.ShapeDtypeStruct((MICRO, TOK, D), BF16),
            jax.ShapeDtypeStruct((MICRO, TOK, TOPK), F32),
            jax.ShapeDtypeStruct((UNITS, D), BF16),
        ),
        in_specs=[vmem] * 4 + [hbm] * 3,
        out_specs=(vmem, vmem, hbm),
        scratch_shapes=[
            pltpu.VMEM((3 * UNITS, D), BF16),
            pltpu.VMEM((MICRO, 128, 256), BF16),
            pltpu.VMEM((MICRO, 15, 16, WIDE), BF16),
            pltpu.VMEM((MICRO, 16, 16, WIDE), BF16),
            pltpu.VMEM((MICRO, 15, 16, HALF), BF16),
            pltpu.VMEM((MICRO, 16, 16, HALF), BF16),
            pltpu.VMEM((MICRO, N_Z, CHUNK_ROWS, CHUNK_COLS), BF16),
            pltpu.VMEM((MICRO, N_Z - 1, CHUNK_ROWS, CHUNK_COLS), BF16),
            pltpu.VMEM((MICRO, N_Y, CHUNK_ROWS, CHUNK_COLS), BF16),
            pltpu.VMEM((MICRO, N_Z, CHUNK_ROWS, CHUNK_COLS), BF16),
            pltpu.VMEM((UNITS, D), BF16),
            pltpu.VMEM((MICRO, 256, UNITS), BF16),
            pltpu.SemaphoreType.DMA((3,)),
            pltpu.SemaphoreType.DMA,
        ] + [pltpu.SemaphoreType.DMA((MICRO,))] * 10,
        compiler_params=pltpu.CompilerParams(
            collective_id=0, has_side_effects=True, vmem_limit_bytes=48 << 20
        ),
    )(
        tokens, cotangent, expert_ids, route_probs,
        gate_weight[0], up_weight[0], down_weight[0],
    )
    return gtok, gprob, gdown[None]


def solution(mesh):
    return jax.shard_map(
        body,
        mesh=mesh,
        in_specs=(
            P(None, "exp", None),
            P(None, "exp", None),
            P(None, "exp", None),
            P(None, "exp", None),
            P("exp", "rep", None),
            P("exp", "rep", None),
            P("exp", "rep", None),
        ),
        out_specs=(P(None, "exp", None), P(None, "exp", None), P("exp", "rep", None)),
        check_vma=False,
    )
```

time: 407 us -> 116 us (0.29)
  the two profiles are of different devices: /device:TPU:8 before, /device:TPU:16 now
where the time goes in v1:
time: 116 us
  Pallas kernels  105 us (91%)
  local copies, waits for them, and re-layouts  9.65 us (8%)
    pallas_call x1, Pallas kernels, body(): pl.pallas_call(kernel, name='expert_backward', out_shape=(jax.ShapeDtypeS...  105 us
    unnamed x19, local copies, waits for them, and re-layouts  9.65 us

profile of v1, /device:TPU:16, one launch (start us, length us, event | category | flops | bytes accessed | tf_op | source)
XLA Modules:
  0.0 115.5 jit_solution(11808254941681463570)
XLA Ops:
  0.6 0.0 copy-start.6
  0.6 0.7 copy-done.6
  1.3 0.0 copy-start.5
  1.3 0.1 copy.11.probs_ref
  1.4 0.6 copy-done.5
  2.0 0.1 copy.10.ids_ref
  2.1 0.0 copy-start
  2.1 1.2 %copy-done = bf16[1,256,2048]{2,1,0:T(8,128)(2,1)S(1)} copy-done((bf16[1,256,2048]{2,1,0:T(8,128)(2,1)S(1)}, bf16[1,256,2048]{2,1,0:T(8,128)(2,1)}, u32[]{:S(2)}) %copy-start) | copy-done | bytes 1048600
  3.3 0.0 copy-start.1
  3.3 1.2 %copy-done.1 = bf16[1,256,2048]{2,1,0:T(8,128)(2,1)S(1)} copy-done((bf16[1,256,2048]{2,1,0:T(8,128)(2,1)S(1)}, bf16[1,256,2048]{2,1,0:T(8,128)(2,1)}, u32[]{:S(2)}) %copy-start.1) | copy-done | bytes 1048600
  4.6 0.0 copy-start.2
  4.6 1.2 %copy-done.2 = bf16[1,256,2048]{2,1,0:T(8,128)(2,1)S(1)} copy-done((bf16[1,256,2048]{2,1,0:T(8,128)(2,1)S(1)}, bf16[1,256,2048]{2,1,0:T(8,128)(2,1)}, u32[]{:S(2)}) %copy-start.2) | copy-done | bytes 1048600
  5.8 0.0 copy-start.3
  5.8 1.0 copy-done.3
  6.8 0.0 copy-start.4
  6.8 1.0 copy-done.4
  7.9 105.2 %expert_backward.1 = (bf16[2,64,2048]{2,1,0:T(8,128)(2,1)S(1)}, f32[2,64,8]{2,1,0:T(8,128)S(1)}, bf16[256,2048]{1,0:T(8,128)(2,1)S(1)}) custom-call(bf16[2,64,2048]{2,1,0:T(8,128)(2,1)S(1)} %copy-done.3, bf16[2,64,2048]{2,1,0:T(8,128)(2,1)S(1)} %copy-done.4, s32[2,64,8]{2,1,0:T(8,128)S(1)} %copy.10.ids_ref, bf16[2,64,8]{2,1,0:T(8,128)(2,1)S(1)} %copy.11.probs_ref, ...), custom_call_target="tpu_custom_call" | custom-call | tf_op jit(solution)/shard_map/expert_backward/pallas_call | solution.py:306
  113.1 0.7 copy.12
  113.8 0.8 copy.15
  114.6 1.0 copy.16
Async XLA Ops:
  0.6 0.7 copy-start.6
  1.3 0.7 copy-start.5
  2.1 1.2 %copy-start = (bf16[1,256,2048]{2,1,0:T(8,128)(2,1)S(1)}, bf16[1,256,2048]{2,1,0:T(8,128)(2,1)}, u32[]{:S(2)}) copy-start(bf16[1,256,2048]{2,1,0:T(8,128)(2,1)} %param.11) | copy-start | bytes 3145732
  3.3 1.2 %copy-start.1 = (bf16[1,256,2048]{2,1,0:T(8,128)(2,1)S(1)}, bf16[1,256,2048]{2,1,0:T(8,128)(2,1)}, u32[]{:S(2)}) copy-start(bf16[1,256,2048]{2,1,0:T(8,128)(2,1)} %param.12) | copy-start | bytes 3145732
  4.6 1.2 %copy-start.2 = (bf16[1,256,2048]{2,1,0:T(8,128)(2,1)S(1)}, bf16[1,256,2048]{2,1,0:T(8,128)(2,1)}, u32[]{:S(2)}) copy-start(bf16[1,256,2048]{2,1,0:T(8,128)(2,1)} %param.13) | copy-start | bytes 3145732
  5.8 1.0 copy-start.3
  6.8 1.0 copy-start.4

commit v2 on v1

v2 whole, which is shorter than its diff:
```python
import jax
import jax.numpy as jnp
from jax import lax
from jax.experimental import pallas as pl
from jax.experimental.pallas import tpu as pltpu
from jax.sharding import PartitionSpec as P

MESH = pl.DeviceIdType.MESH
FF = 1536
TOPK = 8
EXPERTS = 128
MICRO = 2
CAP = 8
N_EXP = 16
N_Z = 12
N_Y = 4
N_K = 4
N_J = N_Z // N_K
PER_GROUP = EXPERTS // N_EXP
TOK = 64
D = 2048
UNITS = 256
WIDE = D + 128
HALF = 1152
CHUNK_ROWS = 32
CHUNK_COLS = 384
BF16 = jnp.bfloat16
F32 = jnp.float32


def flip(a, d):
    out = 0
    for bit in (1, 2, 4, 8):
        out = out + ((a // bit + d // bit) % 2) * bit
    return out


def kernel(
    tok_hbm, cot_hbm, ids_hbm, probs_hbm, gate_hbm, up_hbm, down_hbm,
    gtok_ref, gprob_ref, gdown_ref,
    rows_ref, ids_ref, probs_ref, weights, pick, send_f, recv_f, send_r, recv_r,
    red, recv_s, part_z, recv_w, part_y, fin, gdown, wact_buf,
    in_sem, w_sem, out_sem,
    sf_sem, rf_sem, sr_sem, rr_sem, s1_sem, r1_sem, s2_sem, r2_sem,
    sy_sem, ry_sem, s3_sem, r3_sem, s4_sem, r4_sem,
):
    rep = lax.axis_index("rep")
    me = lax.axis_index("exp")
    z = rep // N_Y
    y_hi = rep % N_Y
    y_lo = me // 8
    core = me % 2
    kind = z % N_K
    turn = z // N_K

    def local_expert(r):
        return r * UNITS // FF

    def rep_of(m, d):
        if m == 0:
            return rep
        step = (d // 8) * (2 * y_lo - 1)
        return z * N_Y + (y_hi + step + N_Y) % N_Y

    def exp_peer(m, p):
        d = p + 1
        return (rep_of(m, d), flip(me, d))

    def z_peer(step):
        return (((z + step + N_Z) % N_Z) * N_Y + y_hi, me)

    def y_peer(q):
        return (z * N_Y + (y_hi + q + 1) % N_Y, me)

    input_copies = [
        pltpu.make_async_copy(src, dst, in_sem.at[i])
        for i, (src, dst) in enumerate((
            (ids_hbm, ids_ref),
            (probs_hbm, probs_ref),
            (tok_hbm.at[0], rows_ref.at[0, pl.ds(0, TOK)]),
            (cot_hbm.at[0], rows_ref.at[0, pl.ds(TOK, TOK)]),
            (tok_hbm.at[1], rows_ref.at[1, pl.ds(0, TOK)]),
            (cot_hbm.at[1], rows_ref.at[1, pl.ds(TOK, TOK)]),
        ))
    ]
    weight_copies = [
        pltpu.make_async_copy(src, weights.at[pl.ds(UNITS * i, UNITS)], w_sem.at[i])
        for i, src in enumerate((gate_hbm, up_hbm, down_hbm))
    ]
    for copy in input_copies:
        copy.start()
    for copy in weight_copies:
        copy.start()

    barrier = pltpu.get_barrier_semaphore()

    def greet(device):
        pl.semaphore_signal(barrier, inc=1, device_id=device, device_id_type=MESH)

    @pl.loop(0, N_EXP - 1)
    def _(p):
        greet(exp_peer(0, p))

    @pl.loop(0, 8)
    def _(p):
        greet(exp_peer(1, p + 7))

    for step in (1, -1, 2, -2, 4, -4):
        greet(z_peer(step))

    @pl.loop(0, N_Y - 1)
    def _(q):
        greet(y_peer(q))

    greeted = (N_EXP - 1) + 8 + 6 + (N_Y - 1)

    row = lax.broadcasted_iota(jnp.int32, (256, 1), 0)
    row_d = (row // 16 + 1) % 16
    row_half = (row // 8) % 2
    row_slot = (row % 8).astype(F32)
    row_exp = flip(me, row_d)
    expert_lane = lax.broadcasted_iota(jnp.int32, (1, EXPERTS), 1)
    expert_row = lax.broadcasted_iota(jnp.int32, (EXPERTS, 1), 0)
    earlier = (
        lax.broadcasted_iota(jnp.int32, (TOK, TOK), 0)
        < lax.broadcasted_iota(jnp.int32, (TOK, TOK), 1)
    ).astype(BF16)

    def prepare(m):
        ids = ids_ref[m]
        probs = probs_ref[m].astype(F32)
        if m == 0:
            group = local_expert(rep)
        else:
            near, far = local_expert(rep), local_expert(rep_of(1, 8))
            group = near + (row_d // 8) * (far - near)
        row_expert = row_exp * PER_GROUP + group
        member = jnp.zeros((256, TOK), F32)
        table = jnp.zeros((EXPERTS, TOK), F32)
        for k in range(TOPK):
            route = ids[k : k + 1]
            member = member + jnp.where(route == row_expert, 1.0, 0.0)
            table = table + jnp.where(route == expert_row, probs[k : k + 1], 0.0)
        before = jnp.dot(member.astype(BF16), earlier, preferred_element_type=F32)
        one_hot = jnp.where(before == row_slot, member, 0.0)
        first = jnp.where(row_half == 0, one_hot, 0.0)
        second = jnp.where(row_half == 1, one_hot, 0.0)
        chosen = jnp.concatenate([first, second], axis=1).astype(BF16)
        pick[m] = chosen

        def put(start, size, out):
            out = out.astype(BF16).reshape(16, 16, size)
            send_f[m, :, :, start : start + size] = out[:15]
            recv_f[m, 15, :, start : start + size] = out[15]

        for start in (0, 1024):
            put(start, 1024, jnp.dot(
                chosen, rows_ref[m, :, start : start + 1024], preferred_element_type=F32
            ))
        put(D, 128, lax.dot_general(
            one_hot.astype(BF16), table.astype(BF16), (((1,), (1,)), ((), ())),
            preferred_element_type=F32,
        ))

    def start_all(count, src, dst, send_sem, recv_sem, peer):
        @pl.loop(0, count)
        def _(i):
            pltpu.make_async_remote_copy(
                src_ref=src(i), dst_ref=dst(i), send_sem=send_sem, recv_sem=recv_sem,
                device_id=peer(i), device_id_type=MESH,
            ).start()

    def wait_for(ref, sem):
        pltpu.make_async_copy(ref, ref, sem).wait()

    def place(i):
        return ((5 + 6 * core) * (i + 1)) % N_EXP - 1

    def send_forward(m):
        start_all(
            15, lambda i: send_f.at[m, place(i)], lambda i: recv_f.at[m, place(i)],
            sf_sem.at[m], rf_sem.at[m], lambda i: exp_peer(m, place(i)),
        )

    def compute(m):
        rows = recv_f[m].reshape(256, WIDE)
        pre = lax.dot_general(
            rows[:, :D], weights[...], (((1,), (1,)), ((), ())), preferred_element_type=F32
        ).reshape(16, 2, 8, 3 * UNITS)
        gate_pre = pre[:, 0, :, :UNITS].reshape(128, UNITS)
        up_pre = pre[:, 0, :, UNITS : 2 * UNITS].reshape(128, UNITS)
        act_grad = pre[:, 1, :, 2 * UNITS :].reshape(128, UNITS)
        mine = (expert_lane == me * PER_GROUP + local_expert(rep)).astype(F32)
        prob = rows[:, D:].astype(F32).reshape(16, 2, 8, 128)[:, 0].reshape(128, 128)
        prob = jnp.sum(prob * mine, axis=1, keepdims=True)
        sigmoid_gate = jax.nn.sigmoid(gate_pre)
        silu_gate = gate_pre * sigmoid_gate
        act = silu_gate * up_pre
        prob_part = jnp.sum(act * act_grad, axis=1, keepdims=True)
        wact = (prob * act).reshape(16, 1, 8, UNITS)
        scaled = prob * act_grad
        gate_grad = scaled * up_pre * sigmoid_gate * (1.0 + gate_pre * (1.0 - sigmoid_gate))
        up_grad = scaled * silu_gate
        wact_buf[m] = (
            jnp.concatenate([jnp.zeros_like(wact), wact], axis=1).reshape(256, UNITS).astype(BF16)
        )
        grads = jnp.concatenate([gate_grad, up_grad], axis=1).astype(BF16)
        left = jnp.dot(grads, weights[: 2 * UNITS, :HALF], preferred_element_type=F32)
        right = jnp.dot(grads, weights[: 2 * UNITS, HALF:], preferred_element_type=F32)
        right = jnp.concatenate([right, prob_part * mine, jnp.zeros((128, 128), F32)], axis=1)
        out = jnp.concatenate(
            [left.reshape(16, 8, HALF), right.reshape(16, 8, HALF)], axis=1
        ).astype(BF16)
        send_r[m] = out[:15]
        recv_r[m, 15] = out[15]

    def send_back(m):
        start_all(
            15, lambda i: send_r.at[m, place(i)], lambda i: recv_r.at[m, place(i)],
            sr_sem.at[m], rr_sem.at[m], lambda i: exp_peer(m, place(i)),
        )

    def combine(m):
        total = lax.dot_general(
            pick[m], recv_r[m].reshape(256, HALF), (((0,), (0,)), ((), ())),
            preferred_element_type=F32,
        ).astype(BF16)
        for c in range(N_Z):
            i, j = c // 3, c % 3
            red[m, i, j] = total[
                CHUNK_ROWS * i : CHUNK_ROWS * (i + 1), CHUNK_COLS * j : CHUNK_COLS * (j + 1)
            ]

    def start_one(src, dst, send_sem, recv_sem, device):
        pltpu.make_async_remote_copy(
            src_ref=src, dst_ref=dst, send_sem=send_sem, recv_sem=recv_sem,
            device_id=device, device_id_type=MESH,
        ).start()

    low, high = pl.ds(0, CHUNK_ROWS // 2), pl.ds(CHUNK_ROWS // 2, CHUNK_ROWS // 2)

    def send_near(m):
        across = (kind + 2) % N_K
        for step, rows in ((2, low), (-2, high)):
            start_one(
                red.at[m, across, :, rows], recv_s.at[m, 2, :, rows],
                s1_sem.at[m], r1_sem.at[m], z_peer(step),
            )
        for slot, step in enumerate((1, -1)):
            start_one(
                red.at[m, (kind + step + N_K) % N_K], recv_s.at[m, slot],
                s1_sem.at[m], r1_sem.at[m], z_peer(step),
            )

    def sum_near(m):
        total = red[m, kind].astype(F32)
        for slot in range(3):
            total = total + recv_s[m, slot].astype(F32)
        part_z[m] = total.astype(BF16)

    def send_far(m):
        for slot, step in enumerate((1, 2)):
            start_one(
                part_z.at[m, (turn + step) % N_J], recv_w.at[m, slot],
                s2_sem.at[m], r2_sem.at[m], z_peer(step * N_K),
            )

    def sum_far(m):
        total = part_z[m, turn].astype(F32)
        for slot in range(N_J - 1):
            total = total + recv_w[m, slot].astype(F32)
        part_y[m, y_hi] = total.astype(BF16)

    def send_y(m):
        start_all(
            N_Y - 1, lambda q: part_y.at[m, y_hi], lambda q: part_y.at[m, y_hi],
            sy_sem.at[m], ry_sem.at[m], y_peer,
        )

    def sum_y(m):
        total = part_y[m, 0].astype(F32)
        for q in range(1, N_Y):
            total = total + part_y[m, q].astype(F32)
        fin[m, kind, turn] = total.astype(BF16)

    def give_far(m):
        for step in (1, 2):
            start_one(
                fin.at[m, kind, turn], fin.at[m, kind, turn],
                s3_sem.at[m], r3_sem.at[m], z_peer(step * N_K),
            )

    def give_near(m):
        for step, rows in ((2, low), (-2, high)):
            start_one(
                fin.at[m, kind, :, rows], fin.at[m, kind, :, rows],
                s4_sem.at[m], r4_sem.at[m], z_peer(step),
            )
        for step in (1, -1):
            start_one(
                fin.at[m, kind], fin.at[m, kind], s4_sem.at[m], r4_sem.at[m], z_peer(step)
            )

    def finish(m):
        for c in range(N_Z):
            i, j = c // 3, c % 3
            top = CHUNK_ROWS * (i % 2)
            col = HALF * (i // 2) + CHUNK_COLS * j
            size = min(CHUNK_COLS, D - col)
            gtok_ref[m, top : top + CHUNK_ROWS, col : col + size] = fin[m, i, j, :, :size]
        ids = ids_ref[m]
        table = jnp.concatenate(
            [fin[m, 2, 2, :, 128:256], fin[m, 3, 2, :, 128:256]], axis=0
        ).astype(F32).T
        gprob_ref[m] = jnp.concatenate(
            [
                jnp.sum(jnp.where(ids[k : k + 1] == expert_row, table, 0.0), axis=0, keepdims=True)
                for k in range(TOPK)
            ],
            axis=0,
        )

    def await_near(m):
        wait_for(recv_s.at[m], r1_sem.at[m])

    def await_far(m):
        wait_for(recv_w.at[m], r2_sem.at[m])

    def await_y(m):
        wait_for(part_y.at[m, pl.ds(0, N_Y - 1)], ry_sem.at[m])

    def await_given_far(m):
        wait_for(recv_w.at[m], r3_sem.at[m])

    def await_given_near(m):
        wait_for(recv_s.at[m], r4_sem.at[m])

    for copy in input_copies[:4]:
        copy.wait()
    prepare(0)
    pl.semaphore_wait(barrier, greeted)
    send_forward(0)
    for copy in input_copies[4:]:
        copy.wait()
    prepare(1)
    send_forward(1)
    for copy in weight_copies:
        copy.wait()

    wait_for(send_f.at[0], rf_sem.at[0])
    compute(0)
    send_back(0)
    wait_for(send_f.at[1], rf_sem.at[1])
    compute(1)
    send_back(1)
    wait_for(send_r.at[0], rr_sem.at[0])
    combine(0)
    send_near(0)

    acts = wact_buf[...].reshape(512, UNITS)
    for part in range(4):
        cols = slice(512 * part, 512 * (part + 1))
        gdown[:, cols] = lax.dot_general(
            acts, recv_f[:, :, :, cols].reshape(512, 512), (((0,), (0,)), ((), ())),
            preferred_element_type=F32,
        ).astype(BF16)
    out_copy = pltpu.make_async_copy(gdown, gdown_ref, out_sem)
    out_copy.start()

    await_near(0)
    sum_near(0)
    send_far(0)
    await_far(0)
    sum_far(0)
    send_y(0)
    wait_for(send_r.at[1], rr_sem.at[1])
    combine(1)
    send_near(1)
    await_y(0)
    sum_y(0)
    give_far(0)
    await_near(1)
    sum_near(1)
    send_far(1)
    await_given_far(0)
    give_near(0)
    await_far(1)
    sum_far(1)
    send_y(1)
    await_given_near(0)
    finish(0)
    await_y(1)
    sum_y(1)
    give_far(1)
    await_given_far(1)
    give_near(1)
    await_given_near(1)
    finish(1)
    out_copy.wait()
    for m in range(MICRO):
        wait_for(send_f.at[m], sf_sem.at[m])
        wait_for(send_r.at[m], sr_sem.at[m])
        wait_for(recv_s.at[m], s1_sem.at[m])
        wait_for(recv_w.at[m], s2_sem.at[m])
        wait_for(part_y.at[m, pl.ds(0, N_Y - 1)], sy_sem.at[m])
        wait_for(recv_w.at[m], s3_sem.at[m])
        wait_for(recv_s.at[m], s4_sem.at[m])


def body(tokens, cotangent, expert_ids, route_probs, gate_weight, up_weight, down_weight):
    vmem = pl.BlockSpec(memory_space=pltpu.VMEM)
    hbm = pl.BlockSpec(memory_space=pltpu.HBM)
    gtok, gprob, gdown = pl.pallas_call(
        kernel,
        name="expert_backward",
        out_shape=(
            jax.ShapeDtypeStruct((MICRO, TOK, D), BF16),
            jax.ShapeDtypeStruct((MICRO, TOPK, TOK), F32),
            jax.ShapeDtypeStruct((UNITS, D), BF16),
        ),
        in_specs=[hbm] * 7,
        out_specs=(vmem, vmem, pl.BlockSpec(memory_space=pl.ANY)),
        scratch_shapes=[
            pltpu.VMEM((MICRO, 2 * TOK, D), BF16),
            pltpu.VMEM((MICRO, TOPK, TOK), jnp.int32),
            pltpu.VMEM((MICRO, TOPK, TOK), BF16),
            pltpu.VMEM((3 * UNITS, D), BF16),
            pltpu.VMEM((MICRO, 256, 128), BF16),
            pltpu.VMEM((MICRO, 15, 16, WIDE), BF16),
            pltpu.VMEM((MICRO, 16, 16, WIDE), BF16),
            pltpu.VMEM((MICRO, 15, 16, HALF), BF16),
            pltpu.VMEM((MICRO, 16, 16, HALF), BF16),
            pltpu.VMEM((MICRO, N_K, N_J, CHUNK_ROWS, CHUNK_COLS), BF16),
            pltpu.VMEM((MICRO, 3, N_J, CHUNK_ROWS, CHUNK_COLS), BF16),
            pltpu.VMEM((MICRO, N_J, CHUNK_ROWS, CHUNK_COLS), BF16),
            pltpu.VMEM((MICRO, N_J - 1, CHUNK_ROWS, CHUNK_COLS), BF16),
            pltpu.VMEM((MICRO, N_Y, CHUNK_ROWS, CHUNK_COLS), BF16),
            pltpu.VMEM((MICRO, N_K, N_J, CHUNK_ROWS, CHUNK_COLS), BF16),
            pltpu.VMEM((UNITS, D), BF16),
            pltpu.VMEM((MICRO, 256, UNITS), BF16),
            pltpu.SemaphoreType.DMA((6,)),
            pltpu.SemaphoreType.DMA((3,)),
            pltpu.SemaphoreType.DMA,
        ] + [pltpu.SemaphoreType.DMA((MICRO,))] * 14,
        compiler_params=pltpu.CompilerParams(
            collective_id=0, has_side_effects=True, vmem_limit_bytes=60 << 20
        ),
    )(
        tokens, cotangent,
        jnp.transpose(expert_ids, (0, 2, 1)), jnp.transpose(route_probs, (0, 2, 1)),
        gate_weight[0], up_weight[0], down_weight[0],
    )
    return gtok, jnp.transpose(gprob, (0, 2, 1)), gdown[None]


def solution(mesh):
    return jax.shard_map(
        body,
        mesh=mesh,
        in_specs=(
            P(None, "exp", None),
            P(None, "exp", None),
            P(None, "exp", None),
            P(None, "exp", None),
            P("exp", "rep", None),
            P("exp", "rep", None),
            P("exp", "rep", None),
        ),
        out_specs=(P(None, "exp", None), P(None, "exp", None), P("exp", "rep", None)),
        check_vma=False,
    )
```

time: 116 us -> 101 us (0.87)
  the two profiles are of different devices: /device:TPU:16 before, /device:TPU:12 now
where the time goes in v2:
time: 101 us
  Pallas kernels  96.7 us (96%)
  local copies, waits for them, and re-layouts  3.55 us (4%)
    pallas_call x1, Pallas kernels, body(): pl.pallas_call(kernel, name='expert_backward', out_shape=(jax.ShapeDtypeS...  96.7 us
    unnamed x7, local copies, waits for them, and re-layouts  3.55 us

profile of v2, /device:TPU:12, one launch (start us, length us, event | category | flops | bytes accessed | tf_op | source)
XLA Modules:
  0.0 100.9 jit_solution(10688268765155711749)
XLA Ops:
  0.6 96.7 %expert_backward.1 = (bf16[2,64,2048]{2,1,0:T(8,128)(2,1)}, f32[2,8,64]{2,1,0:T(8,128)}, bf16[256,2048]{1,0:T(8,128)(2,1)}) custom-call(bf16[2,64,2048]{2,1,0:T(8,128)(2,1)} %tok_hbm.1, bf16[2,64,2048]{2,1,0:T(8,128)(2,1)} %cot_hbm.1, s32[2,8,64]{2,1,0:T(8,128)} %bitcast.11, bf16[2,8,64]{2,1,0:T(8,128)(2,1)} %bitcast.13, bf16[256,2048]{1,0:T(8,128)(2,1)} %bitcast.7, ...), custom_call_target="tpu_custom_call" | custom-call | tf_op jit(solution)/shard_map/expert_backward/pallas_call | solution.py:413
  97.3 0.0 copy-start
  97.3 0.0 copy-start.1
  97.3 2.0 %copy.13 = bf16[2,64,2048]{2,1,0:T(8,128)(2,1)} copy(bf16[2,64,2048]{2,1,0:T(8,128)(2,1)} %get-tuple-element.12) | data formatting | bytes 1048576
  99.3 0.0 copy-done.1
  99.3 0.6 copy.14
  99.9 0.0 copy-done
  99.9 1.0 copy.15
Async XLA Ops:
  97.3 2.6 %copy-start = (bf16[256,2048]{1,0:T(8,128)(2,1)S(1)}, bf16[256,2048]{1,0:T(8,128)(2,1)}, u32[]{:S(2)}) copy-start(bf16[256,2048]{1,0:T(8,128)(2,1)} %get-tuple-element.8) | copy-start | bytes 3145732
  97.3 2.0 %copy-start.1 = (f32[2,8,64]{2,1,0:T(8,128)S(1)}, f32[2,8,64]{2,1,0:T(8,128)}, u32[]{:S(2)}) copy-start(f32[2,8,64]{2,1,0:T(8,128)} %get-tuple-element.7) | copy-start | bytes 12292

commit v3 on v2

--- a/solution.py
+++ b/solution.py
@@ -15,15 +15,16 @@
 N_Z = 12
 N_Y = 4
 N_K = 4
-N_J = N_Z // N_K
+N_T = N_Z // N_K
+N_C = 9
+N_OWN = N_C // N_T
 PER_GROUP = EXPERTS // N_EXP
 TOK = 64
 D = 2048
 UNITS = 256
 WIDE = D + 128
 HALF = 1152
-CHUNK_ROWS = 32
-CHUNK_COLS = 384
+CHUNK = (32, 128)
 BF16 = jnp.bfloat16
 F32 = jnp.float32
 
@@ -39,10 +40,10 @@
     tok_hbm, cot_hbm, ids_hbm, probs_hbm, gate_hbm, up_hbm, down_hbm,
     gtok_ref, gprob_ref, gdown_ref,
     rows_ref, ids_ref, probs_ref, weights, pick, send_f, recv_f, send_r, recv_r,
-    red, recv_s, part_z, recv_w, part_y, fin, gdown, wact_buf,
+    red, recv_s, part_z, recv_w, fin, gdown, wact_buf,
     in_sem, w_sem, out_sem,
     sf_sem, rf_sem, sr_sem, rr_sem, s1_sem, r1_sem, s2_sem, r2_sem,
-    sy_sem, ry_sem, s3_sem, r3_sem, s4_sem, r4_sem,
+    s3_sem, r3_sem, s4_sem, r4_sem,
 ):
     rep = lax.axis_index("rep")
     me = lax.axis_index("exp")
@@ -56,10 +57,11 @@
     def local_expert(r):
         return r * UNITS // FF
 
+    def far_side(m, d):
+        return (d // 8) * ((d + m) % 2)
+
     def rep_of(m, d):
-        if m == 0:
-            return rep
-        step = (d // 8) * (2 * y_lo - 1)
+        step = far_side(m, d) * (2 * y_lo - 1)
         return z * N_Y + (y_hi + step + N_Y) % N_Y
 
     def exp_peer(m, p):
@@ -69,8 +71,9 @@
     def z_peer(step):
         return (((z + step + N_Z) % N_Z) * N_Y + y_hi, me)
 
-    def y_peer(q):
-        return (z * N_Y + (y_hi + q + 1) % N_Y, me)
+    def kin(q):
+        to_turn, to_y = (turn + q // N_Y) % N_T, (y_hi + q) % N_Y
+        return ((to_turn * N_K + kind) * N_Y + to_y, me), to_turn * N_OWN + to_y, to_y < N_OWN
 
     input_copies = [
         pltpu.make_async_copy(src, dst, in_sem.at[i])
@@ -101,18 +104,18 @@
     def _(p):
         greet(exp_peer(0, p))
 
-    @pl.loop(0, 8)
+    @pl.loop(7, N_EXP - 1)
     def _(p):
-        greet(exp_peer(1, p + 7))
-
-    for step in (1, -1, 2, -2, 4, -4):
+        greet(exp_peer(1, p))
+
+    for step in (1, -1, 2, -2):
         greet(z_peer(step))
 
-    @pl.loop(0, N_Y - 1)
+    @pl.loop(1, N_T * N_Y)
     def _(q):
-        greet(y_peer(q))
-
-    greeted = (N_EXP - 1) + 8 + 6 + (N_Y - 1)
+        greet(kin(q)[0])
+
+    greeted = (N_EXP - 1) + 8 + 4 + (N_T * N_Y - 1)
 
     row = lax.broadcasted_iota(jnp.int32, (256, 1), 0)
     row_d = (row // 16 + 1) % 16
@@ -129,11 +132,8 @@
     def prepare(m):
         ids = ids_ref[m]
         probs = probs_ref[m].astype(F32)
-        if m == 0:
-            group = local_expert(rep)
-        else:
-            near, far = local_expert(rep), local_expert(rep_of(1, 8))
-            group = near + (row_d // 8) * (far - near)
+        near, far = local_expert(rep), local_expert(rep_of(m, 9 - m))
+        group = near + far_side(m, row_d) * (far - near)
         row_expert = row_exp * PER_GROUP + group
         member = jnp.zeros((256, TOK), F32)
         table = jnp.zeros((EXPERTS, TOK), F32)
@@ -225,11 +225,9 @@
             pick[m], recv_r[m].reshape(256, HALF), (((0,), (0,)), ((), ())),
             preferred_element_type=F32,
         ).astype(BF16)
-        for c in range(N_Z):
-            i, j = c // 3, c % 3
-            red[m, i, j] = total[
-                CHUNK_ROWS * i : CHUNK_ROWS * (i + 1), CHUNK_COLS * j : CHUNK_COLS * (j + 1)
-            ]
+        for k in range(N_K):
+            for c in range(N_C):
+                red[m, k, c] = total[32 * k : 32 * (k + 1), 128 * c : 128 * (c + 1)]
 
     def start_one(src, dst, send_sem, recv_sem, device):
         pltpu.make_async_remote_copy(
@@ -237,13 +235,15 @@
             device_id=device, device_id_type=MESH,
         ).start()
 
-    low, high = pl.ds(0, CHUNK_ROWS // 2), pl.ds(CHUNK_ROWS // 2, CHUNK_ROWS // 2)
+    low, high = pl.ds(0, 5), pl.ds(5, N_C - 5)
+    owner = y_hi < N_OWN
+    own = turn * N_OWN + y_hi
 
     def send_near(m):
         across = (kind + 2) % N_K
-        for step, rows in ((2, low), (-2, high)):
+        for step, part in ((2, low), (-2, high)):
             start_one(
-                red.at[m, across, :, rows], recv_s.at[m, 2, :, rows],
+                red.at[m, across, part], recv_s.at[m, 2, part],
                 s1_sem.at[m], r1_sem.at[m], z_peer(step),
             )
         for slot, step in enumerate((1, -1)):
@@ -252,48 +252,59 @@
                 s1_sem.at[m], r1_sem.at[m], z_peer(step),
             )
 
-    def sum_near(m):
+    def await_near(m):
+        wait_for(recv_s.at[m], r1_sem.at[m])
         total = red[m, kind].astype(F32)
         for slot in range(3):
             total = total + recv_s[m, slot].astype(F32)
         part_z[m] = total.astype(BF16)
 
-    def send_far(m):
-        for slot, step in enumerate((1, 2)):
+    def send_kin(m):
+        @pl.loop(1, N_T * N_Y)
+        def _(q):
+            device, chunk, owns = kin(q)
+
+            @pl.when(owns)
+            def _():
+                start_one(
+                    part_z.at[m, chunk], recv_w.at[m, q - 1], s2_sem.at[m], r2_sem.at[m], device
+                )
+
+    def await_kin(m):
+        @pl.when(owner)
+        def _():
+            wait_for(recv_w.at[m], r2_sem.at[m])
+            total = part_z[m, own].astype(F32)
+            for slot in range(N_T * N_Y - 1):
+                total = total + recv_w[m, slot].astype(F32)
+            fin[m, kind, own] = total.astype(BF16)
+
+    def give_kin(m):
+        @pl.when(owner)
+        def _():
+            @pl.loop(1, N_T * N_Y)
+            def _(q):
+                start_one(
+                    fin.at[m, kind, own], fin.at[m, kind, own],
+                    s3_sem.at[m], r3_sem.at[m], kin(q)[0],
+                )
+
+    def wait_but_own(ref, sem):
+        @pl.when(owner)
+        def _():
+            wait_for(ref.at[pl.ds(0, N_C - 1)], sem)
+
+        @pl.when(jnp.logical_not(owner))
+        def _():
+            wait_for(ref.at[pl.ds(0, N_C)], sem)
+
+    def await_given_kin(m):
+        wait_but_own(recv_w.at[m], r3_sem.at[m])
+
+    def give_near(m):
+        for step, part in ((2, low), (-2, high)):
             start_one(
-                part_z.at[m, (turn + step) % N_J], recv_w.at[m, slot],
-                s2_sem.at[m], r2_sem.at[m], z_peer(step * N_K),
-            )
-
-    def sum_far(m):
-        total = part_z[m, turn].astype(F32)
-        for slot in range(N_J - 1):
-            total = total + recv_w[m, slot].astype(F32)
-        part_y[m, y_hi] = total.astype(BF16)
-
-    def send_y(m):
-        start_all(
-            N_Y - 1, lambda q: part_y.at[m, y_hi], lambda q: part_y.at[m, y_hi],
-            sy_sem.at[m], ry_sem.at[m], y_peer,
-        )
-
-    def sum_y(m):
-        total = part_y[m, 0].astype(F32)
-        for q in range(1, N_Y):
-            total = total + part_y[m, q].astype(F32)
-        fin[m, kind, turn] = total.astype(BF16)
-
-    def give_far(m):
-        for step in (1, 2):
-            start_one(
-                fin.at[m, kind, turn], fin.at[m, kind, turn],
-                s3_sem.at[m], r3_sem.at[m], z_peer(step * N_K),
-            )
-
-    def give_near(m):
-        for step, rows in ((2, low), (-2, high)):
-            start_one(
-                fin.at[m, kind, :, rows], fin.at[m, kind, :, rows],
+                fin.at[m, kind, part], fin.at[m, kind, part],
                 s4_sem.at[m], r4_sem.at[m], z_peer(step),
             )
         for step in (1, -1):
@@ -301,17 +312,19 @@
                 fin.at[m, kind], fin.at[m, kind], s4_sem.at[m], r4_sem.at[m], z_peer(step)
             )
 
+    def await_given_near(m):
+        wait_for(recv_s.at[m], r4_sem.at[m])
+
     def finish(m):
-        for c in range(N_Z):
-            i, j = c // 3, c % 3
-            top = CHUNK_ROWS * (i % 2)
-            col = HALF * (i // 2) + CHUNK_COLS * j
-            size = min(CHUNK_COLS, D - col)
-            gtok_ref[m, top : top + CHUNK_ROWS, col : col + size] = fin[m, i, j, :, :size]
+        for k in range(N_K):
+            top = 32 * (k % 2)
+            for c in range(N_C):
+                col = HALF * (k // 2) + 128 * c
+                if col < D:
+                    gtok_ref[m, top : top + 32, col : col + 128] = fin[m, k, c]
         ids = ids_ref[m]
-        table = jnp.concatenate(
-            [fin[m, 2, 2, :, 128:256], fin[m, 3, 2, :, 128:256]], axis=0
-        ).astype(F32).T
+        place_of = (D - HALF) // 128
+        table = jnp.concatenate([fin[m, 2, place_of], fin[m, 3, place_of]], axis=0).astype(F32).T
         gprob_ref[m] = jnp.concatenate(
             [
                 jnp.sum(jnp.where(ids[k : k + 1] == expert_row, table, 0.0), axis=0, keepdims=True)
@@ -319,21 +332,6 @@
             ],
             axis=0,
         )
-
-    def await_near(m):
-        wait_for(recv_s.at[m], r1_sem.at[m])
-
-    def await_far(m):
-        wait_for(recv_w.at[m], r2_sem.at[m])
-
-    def await_y(m):
-        wait_for(part_y.at[m, pl.ds(0, N_Y - 1)], ry_sem.at[m])
-
-    def await_given_far(m):
-        wait_for(recv_w.at[m], r3_sem.at[m])
-
-    def await_given_near(m):
-        wait_for(recv_s.at[m], r4_sem.at[m])
 
     for copy in input_copies[:4]:
         copy.wait()
@@ -343,6 +341,7 @@
     for copy in input_copies[4:]:
         copy.wait()
     prepare(1)
+    wait_for(send_f.at[0], sf_sem.at[0])
     send_forward(1)
     for copy in weight_copies:
         copy.wait()
@@ -368,42 +367,35 @@
     out_copy.start()
 
     await_near(0)
-    sum_near(0)
-    send_far(0)
-    await_far(0)
-    sum_far(0)
-    send_y(0)
+    send_kin(0)
     wait_for(send_r.at[1], rr_sem.at[1])
     combine(1)
     send_near(1)
-    await_y(0)
-    sum_y(0)
-    give_far(0)
+    await_kin(0)
+    give_kin(0)
     await_near(1)
-    sum_near(1)
-    send_far(1)
-    await_given_far(0)
+    send_kin(1)
+    await_given_kin(0)
     give_near(0)
-    await_far(1)
-    sum_far(1)
-    send_y(1)
+    await_kin(1)
+    give_kin(1)
     await_given_near(0)
     finish(0)
-    await_y(1)
-    sum_y(1)
-    give_far(1)
-    await_given_far(1)
+    await_given_kin(1)
     give_near(1)
     await_given_near(1)
     finish(1)
     out_copy.wait()
+    wait_for(send_f.at[1], sf_sem.at[1])
     for m in range(MICRO):
-        wait_for(send_f.at[m], sf_sem.at[m])
         wait_for(send_r.at[m], sr_sem.at[m])
         wait_for(recv_s.at[m], s1_sem.at[m])
-        wait_for(recv_w.at[m], s2_sem.at[m])
-        wait_for(part_y.at[m, pl.ds(0, N_Y - 1)], sy_sem.at[m])
-        wait_for(recv_w.at[m], s3_sem.at[m])
+        wait_but_own(recv_w.at[m], s2_sem.at[m])
+
+        @pl.when(owner)
+        def _():
+            wait_for(recv_w.at[m], s3_sem.at[m])
+
         wait_for(recv_s.at[m], s4_sem.at[m])
 
 
@@ -430,18 +422,17 @@
             pltpu.VMEM((MICRO, 16, 16, WIDE), BF16),
             pltpu.VMEM((MICRO, 15, 16, HALF), BF16),
             pltpu.VMEM((MICRO, 16, 16, HALF), BF16),
-            pltpu.VMEM((MICRO, N_K, N_J, CHUNK_ROWS, CHUNK_COLS), BF16),
-            pltpu.VMEM((MICRO, 3, N_J, CHUNK_ROWS, CHUNK_COLS), BF16),
-            pltpu.VMEM((MICRO, N_J, CHUNK_ROWS, CHUNK_COLS), BF16),
-            pltpu.VMEM((MICRO, N_J - 1, CHUNK_ROWS, CHUNK_COLS), BF16),
-            pltpu.VMEM((MICRO, N_Y, CHUNK_ROWS, CHUNK_COLS), BF16),
-            pltpu.VMEM((MICRO, N_K, N_J, CHUNK_ROWS, CHUNK_COLS), BF16),
+            pltpu.VMEM((MICRO, N_K, N_C, *CHUNK), BF16),
+            pltpu.VMEM((MICRO, 3, N_C, *CHUNK), BF16),
+            pltpu.VMEM((MICRO, N_C, *CHUNK), BF16),
+            pltpu.VMEM((MICRO, N_T * N_Y - 1, *CHUNK), BF16),
+            pltpu.VMEM((MICRO, N_K, N_C, *CHUNK), BF16),
             pltpu.VMEM((UNITS, D), BF16),
             pltpu.VMEM((MICRO, 256, UNITS), BF16),
             pltpu.SemaphoreType.DMA((6,)),
             pltpu.SemaphoreType.DMA((3,)),
             pltpu.SemaphoreType.DMA,
-        ] + [pltpu.SemaphoreType.DMA((MICRO,))] * 14,
+        ] + [pltpu.SemaphoreType.DMA((MICRO,))] * 12,
         compiler_params=pltpu.CompilerParams(
             collective_id=0, has_side_effects=True, vmem_limit_bytes=60 << 20
         ),

time: 101 us -> 97.3 us (0.963)
  the two profiles are of different devices: /device:TPU:12 before, /device:TPU:64 now
where the time goes in v3:
time: 97.3 us; the launch traced here: 97.2 us
  Pallas kernels  93 us (96%)
  local copies, waits for them, and re-layouts  3.55 us (4%)
    pallas_call x1, Pallas kernels, body(): pl.pallas_call(kernel, name='expert_backward', out_shape=(jax.ShapeDtypeS...  93 us
    unnamed x7, local copies, waits for them, and re-layouts  3.55 us

profile of v3, /device:TPU:64, one launch (start us, length us, event | category | flops | bytes accessed | tf_op | source)
XLA Modules:
  0.0 97.2 jit_solution(2714627744729279525)
XLA Ops:
  0.6 93.0 %expert_backward.1 = (bf16[2,64,2048]{2,1,0:T(8,128)(2,1)}, f32[2,8,64]{2,1,0:T(8,128)}, bf16[256,2048]{1,0:T(8,128)(2,1)}) custom-call(bf16[2,64,2048]{2,1,0:T(8,128)(2,1)} %tok_hbm.1, bf16[2,64,2048]{2,1,0:T(8,128)(2,1)} %cot_hbm.1, s32[2,8,64]{2,1,0:T(8,128)} %bitcast.11, bf16[2,8,64]{2,1,0:T(8,128)(2,1)} %bitcast.13, bf16[256,2048]{1,0:T(8,128)(2,1)} %bitcast.7, ...), custom_call_target="tpu_custom_call" | custom-call | tf_op jit(solution)/shard_map/expert_backward/pallas_call | solution.py:405
  93.6 0.0 copy-start
  93.6 0.0 copy-start.1
  93.6 2.0 %copy.13 = bf16[2,64,2048]{2,1,0:T(8,128)(2,1)} copy(bf16[2,64,2048]{2,1,0:T(8,128)(2,1)} %get-tuple-element.12) | data formatting | bytes 1048576
  95.6 0.0 copy-done.1
  95.6 0.6 copy.14
  96.2 0.0 copy-done
  96.2 1.0 copy.15
Async XLA Ops:
  93.6 2.6 %copy-start = (bf16[256,2048]{1,0:T(8,128)(2,1)S(1)}, bf16[256,2048]{1,0:T(8,128)(2,1)}, u32[]{:S(2)}) copy-start(bf16[256,2048]{1,0:T(8,128)(2,1)} %get-tuple-element.8) | copy-start | bytes 3145732
  93.6 2.0 %copy-start.1 = (f32[2,8,64]{2,1,0:T(8,128)S(1)}, f32[2,8,64]{2,1,0:T(8,128)}, u32[]{:S(2)}) copy-start(f32[2,8,64]{2,1,0:T(8,128)} %get-tuple-element.7) | copy-start | bytes 12292

commit v4 on v3

--- a/solution.py
+++ b/solution.py
@@ -260,8 +260,9 @@
         part_z[m] = total.astype(BF16)
 
     def send_kin(m):
-        @pl.loop(1, N_T * N_Y)
-        def _(q):
+        @pl.loop(0, N_T * N_Y - 1)
+        def _(i):
+            q = (i + 5) % (N_T * N_Y - 1) + 1
             device, chunk, owns = kin(q)
 
             @pl.when(owns)
@@ -282,8 +283,9 @@
     def give_kin(m):
         @pl.when(owner)
         def _():
-            @pl.loop(1, N_T * N_Y)
-            def _(q):
+            @pl.loop(0, N_T * N_Y - 1)
+            def _(i):
+                q = (i + 5) % (N_T * N_Y - 1) + 1
                 start_one(
                     fin.at[m, kind, own], fin.at[m, kind, own],
                     s3_sem.at[m], r3_sem.at[m], kin(q)[0],
@@ -397,6 +399,35 @@
             wait_for(recv_w.at[m], s3_sem.at[m])
 
         wait_for(recv_s.at[m], s4_sem.at[m])
+
+
+def hand_on_kernel(*refs):
+    sources, results, sem = refs[:3], refs[3:6], refs[6]
+    copies = []
+    for source, result in zip(sources, results):
+        rows = source.shape[0]
+        pieces = 4 if rows == UNITS else rows
+        for p in range(pieces):
+            part = pl.ds(p * (rows // pieces), rows // pieces)
+            copies.append(
+                pltpu.make_async_copy(source.at[part], result.at[part], sem.at[len(copies)])
+            )
+    for copy in copies:
+        copy.start()
+    for copy in copies:
+        copy.wait()
+
+
+def hand_on(*arrays):
+    anywhere = pl.BlockSpec(memory_space=pl.ANY)
+    return pl.pallas_call(
+        hand_on_kernel,
+        name="hand_on",
+        out_shape=tuple(jax.ShapeDtypeStruct(a.shape, a.dtype) for a in arrays),
+        in_specs=[anywhere] * 3,
+        out_specs=(anywhere,) * 3,
+        scratch_shapes=[pltpu.SemaphoreType.DMA((8,))],
+    )(*arrays)
 
 
 def body(tokens, cotangent, expert_ids, route_probs, gate_weight, up_weight, down_weight):
@@ -441,6 +472,7 @@
         jnp.transpose(expert_ids, (0, 2, 1)), jnp.transpose(route_probs, (0, 2, 1)),
         gate_weight[0], up_weight[0], down_weight[0],
     )
+    gtok, gprob, gdown = hand_on(gtok, gprob, gdown)
     return gtok, jnp.transpose(gprob, (0, 2, 1)), gdown[None]
 
 

time: 97.3 us -> 143 us (1.47)
  the two profiles are of different devices: /device:TPU:64 before, /device:TPU:2 now
where the time goes in v4:
time: 143 us; the launch traced here: 142 us
  Pallas kernels  142 us (99%)
    pallas_call x1, Pallas kernels, body(): pl.pallas_call(kernel, name='expert_backward', out_shape=(jax.ShapeDtypeS...  92.7 us
    pallas_call x1, Pallas kernels, hand_on(): pl.pallas_call(hand_on_kernel, name='hand_on', out_shape=tuple((jax.Shape...  49.1 us

profile of v4, /device:TPU:2, one launch (start us, length us, event | category | flops | bytes accessed | tf_op | source)
XLA Modules:
  0.0 142.4 jit_solution(16842483187400785855)
XLA Ops:
  0.6 92.7 %expert_backward.1 = (bf16[2,64,2048]{2,1,0:T(8,128)(2,1)}, f32[2,8,64]{2,1,0:T(8,128)}, bf16[256,2048]{1,0:T(8,128)(2,1)}) custom-call(bf16[2,64,2048]{2,1,0:T(8,128)(2,1)} %tok_hbm.1, bf16[2,64,2048]{2,1,0:T(8,128)(2,1)} %cot_hbm.1, s32[2,8,64]{2,1,0:T(8,128)} %bitcast.10, bf16[2,8,64]{2,1,0:T(8,128)(2,1)} %bitcast.11, bf16[256,2048]{1,0:T(8,128)(2,1)} %bitcast.7, ...), custom_call_target="tpu_custom_call" | custom-call | tf_op jit(solution)/shard_map/expert_backward/pallas_call | solution.py:436
  93.3 49.1 %hand_on.1 = (bf16[2,64,2048]{2,1,0:T(8,128)(2,1)}, f32[2,8,64]{2,1,0:T(8,128)}, bf16[256,2048]{1,0:T(8,128)(2,1)}) custom-call(bf16[2,64,2048]{2,1,0:T(8,128)(2,1)} %get-tuple-element.9.refs_0_, f32[2,8,64]{2,1,0:T(8,128)} %get-tuple-element.10.refs_1_, bf16[256,2048]{1,0:T(8,128)(2,1)} %get-tuple-element.11.refs_2_), custom_call_target="tpu_custom_call" | custom-call | tf_op jit(solution)/shard_map/hand_on/pallas_call | solution.py:423
